TPU v7x, 32 devices: a whole 2x2x4 slice. The times are simulated.
32 devices in a mesh: dp: 8 (over y, x, core), cent: 4 (over z).
Axes of the slice: x: 2, y: 2, z: 4, core: 2. Of those that a mesh axis runs over, the one named last changes fastest.
Arguments:
- points: bfloat16 [16384, 1024], P(('dp', 'cent')), may hold values from -8 to 8
- fine_assign: int32 [16384], P(('dp', 'cent')), may hold values from 0 to 4095, as said below
- coarse_assign: int32 [4096], P(('dp', 'cent')), may hold values from 0 to 4095, as said below
Outputs:
- spread: float32 [16384], P(('dp', 'cent'))
- fine_centroids: bfloat16 [4096, 1024], P(('dp', 'cent'))
- coarse_centroids: bfloat16 [4096, 1024], P('cent')
Inputs may be any that keep to these rules, and one draw needn't show every extreme that they name: `fine_assign`: devices are numbered with dp slowest; device s holds points s * 512 to (s + 1) * 512 - 1 and fine centroids s * 128 to (s + 1) * 128 - 1. At most 32 of the points of one device are assigned into any one block b * 128 to (b + 1) * 128 - 1 of fine centroids, and in every draw some block receives exactly 32 points from every device. `coarse_assign`: the 128 fine centroids of one device name at most 64 coarse centroids of any one block c * 1024 to (c + 1) * 1024 - 1, and in every draw some block receives exactly 64 from every device.
All inputs are finite; a program needn't handle non-finite values.
Results may differ from a plain program's by a relative error of at most 0.014.
Values may be sent and summed in bfloat16 or wider, within the bound.
A program may use at most 64 MiB of HBM per device.

v0:
```python
import jax
import jax.numpy as jnp
from jax import lax
from jax.sharding import PartitionSpec as P

FINE_DEV = 128
COARSE = 4096


def place_rows(targets, total_slots, capacity):
    count = targets.shape[0]
    ranking = jnp.argsort(targets, stable=True)
    sorted_targets = targets[ranking]
    leading = jnp.searchsorted(sorted_targets, sorted_targets, side="left")
    sorted_rank = jnp.arange(count, dtype=jnp.int32) - leading
    within = jnp.zeros((count,), jnp.int32).at[ranking].set(sorted_rank)
    destination = targets * capacity + within
    slot_source = (
        jnp.full((total_slots,), count, jnp.int32)
        .at[destination]
        .set(jnp.arange(count, dtype=jnp.int32))
    )
    return (destination, slot_source)


def body(points, fine_assign, coarse_assign):
    n_data = lax.axis_size("dp")
    n_cent = lax.axis_size("cent")
    sources = n_data * n_cent
    p_rows, width = points.shape
    capacity = max(2, 2 * p_rows // sources)
    owners = fine_assign // FINE_DEV
    destination, slot_source = place_rows(owners, sources * capacity, capacity)
    send_rows = jnp.take(points, slot_source, axis=0, mode="fill", fill_value=0).reshape(
        n_data, n_cent, capacity, width
    )
    send_ids = jnp.take(fine_assign % FINE_DEV, slot_source, mode="fill", fill_value=-1).reshape(
        n_data, n_cent, capacity
    )
    got_rows, got_ids = (
        lax.all_to_all(
            lax.all_to_all(send_rows, "dp", split_axis=0, concat_axis=0, tiled=True),
            "cent",
            split_axis=1,
            concat_axis=1,
            tiled=True,
        ),
        lax.all_to_all(
            lax.all_to_all(send_ids, "dp", split_axis=0, concat_axis=0, tiled=True),
            "cent",
            split_axis=1,
            concat_axis=1,
            tiled=True,
        ),
    )
    flat_rows = got_rows.reshape(-1, width)
    flat_ids = got_ids.reshape(-1)
    members = flat_ids[None, :] == jnp.arange(FINE_DEV, dtype=jnp.int32)[:, None]
    one_hot = members.astype(jnp.bfloat16)
    fine_sums = jnp.dot(one_hot, flat_rows, preferred_element_type=jnp.float32)
    fine_counts = jnp.sum(members.astype(jnp.float32), axis=1)
    fine_centroids = (fine_sums / jnp.maximum(fine_counts, 1.0)[:, None]).astype(jnp.bfloat16)
    selected = lax.dot_general(
        one_hot, fine_centroids, (((0,), (0,)), ((), ())), preferred_element_type=jnp.float32
    )
    returned = lax.all_to_all(
        lax.all_to_all(
            selected.astype(jnp.bfloat16).reshape(n_data, n_cent, capacity, width),
            "dp",
            split_axis=0,
            concat_axis=0,
            tiled=True,
        ),
        "cent",
        split_axis=1,
        concat_axis=1,
        tiled=True,
    )
    nearest = jnp.take(returned.reshape(-1, width), destination, axis=0)
    spread = jnp.mean(jnp.square(points.astype(jnp.float32) - nearest.astype(jnp.float32)), axis=-1)
    block = COARSE // n_cent
    capacity_two = max(2, 2 * FINE_DEV // n_cent)
    coarse_owner = coarse_assign // block
    unused_dest, coarse_source = place_rows(coarse_owner, n_cent * capacity_two, capacity_two)
    send_fine = jnp.take(fine_centroids, coarse_source, axis=0, mode="fill", fill_value=0).reshape(
        n_cent, capacity_two, width
    )
    send_labels = jnp.take(
        coarse_assign % block, coarse_source, mode="fill", fill_value=-1
    ).reshape(n_cent, capacity_two)
    got_fine, got_labels = (
        lax.all_to_all(send_fine, "cent", split_axis=0, concat_axis=0, tiled=True),
        lax.all_to_all(send_labels, "cent", split_axis=0, concat_axis=0, tiled=True),
    )
    coarse_members = got_labels.reshape(-1)[None, :] == jnp.arange(block, dtype=jnp.int32)[:, None]
    partial_value = jnp.dot(
        coarse_members.astype(jnp.bfloat16),
        got_fine.reshape(-1, width),
        preferred_element_type=jnp.float32,
    )
    tally = jnp.sum(coarse_members.astype(jnp.float32), axis=1)
    totals, tallies = (
        lax.psum(partial_value.astype(jnp.bfloat16), "dp").astype(jnp.float32),
        lax.psum(tally.astype(jnp.bfloat16), "dp").astype(jnp.float32),
    )
    coarse_centroids = (totals / jnp.maximum(tallies, 1.0)[:, None]).astype(jnp.bfloat16)
    return (spread, fine_centroids, coarse_centroids)


def solution(mesh):
    placed = (P(("dp", "cent"), None), P(("dp", "cent")), P(("dp", "cent")))
    return jax.shard_map(
        body,
        mesh=mesh,
        in_specs=placed,
        out_specs=(P(("dp", "cent")), P(("dp", "cent"), None), P("cent", None)),
        check_vma=False,
    )
```

profile of v0, /device:TPU:1, one launch (start us, length us, event | category | flops | bytes accessed | tf_op | source)
XLA Modules:
  0.0 309.1 jit_solution(12972192472399361235)
XLA Ops:
  7.9 3.8 %sort.34 = (s32[512]{0:T(512)}, s32[512]{0:T(512)S(1)}) sort(s32[512]{0:T(512)S(1)} %get-tuple-element.198, s32[512]{0:T(512)S(1)} %iota.28), dimensions={0}, to_apply=%region_0.1 | sort | flops 4608 | bytes 8192 | tf_op jit(solution)/shard_map/jit(argsort)/sort | solution.py:12
  15.2 35.9 %while.50 = (s32[]{:T(128)}, u32[512]{0:T(512)S(1)}, u32[512]{0:T(512)S(1)}, s32[512]{0:T(512)S(1)}, s32[]{:T(128)}, /*index=5*/s32[]{:T(128)}, s32[]{}) while((s32[]{:T(128)}, u32[512]{0:T(512)S(1)}, u32[512]{0:T(512)S(1)}, s32[512]{0:T(512)S(1)}, s32[]{:T(128)}, /*index=5*/s32[]{:T(128)}, s32[]{}) %tuple.75), condition=%wide.region_2.3_spmd.clone, body=%wide.region_1.2_spmd.clone.sunk | while | flops 10244 | bytes 40037 | solution.py:14
  15.2 3.5 %gather_fusion = s32[512]{0:T(512)S(1)} fusion(s32[512]{0:T(512)S(1)} %get-tuple-element.276, u32[1024]{0:T(1024)S(1)} %pad_clamp_fusion.8), kind=kCustom, calls=%fused_computation.clone.clone.1 | custom fusion | bytes 6144 | tf_op jit(solution)/shard_map/jit(searchsorted)/jit(_searchsorted_scan_impl)/vmap(jit(_searchsorted_scan_impl))/while/body/eval_jaxpr/gather | solution.py:14
  18.8 3.5 %gather_fusion = s32[512]{0:T(512)S(1)} fusion(s32[512]{0:T(512)S(1)} %get-tuple-element.276, u32[1024]{0:T(1024)S(1)} %pad_clamp_fusion.8), kind=kCustom, calls=%fused_computation.clone.clone.1 | custom fusion | bytes 6144 | tf_op jit(solution)/shard_map/jit(searchsorted)/jit(_searchsorted_scan_impl)/vmap(jit(_searchsorted_scan_impl))/while/body/eval_jaxpr/gather | solution.py:14
  22.4 3.5 %gather_fusion = s32[512]{0:T(512)S(1)} fusion(s32[512]{0:T(512)S(1)} %get-tuple-element.276, u32[1024]{0:T(1024)S(1)} %pad_clamp_fusion.8), kind=kCustom, calls=%fused_computation.clone.clone.1 | custom fusion | bytes 6144 | tf_op jit(solution)/shard_map/jit(searchsorted)/jit(_searchsorted_scan_impl)/vmap(jit(_searchsorted_scan_impl))/while/body/eval_jaxpr/gather | solution.py:14
  26.0 3.5 %gather_fusion = s32[512]{0:T(512)S(1)} fusion(s32[512]{0:T(512)S(1)} %get-tuple-element.276, u32[1024]{0:T(1024)S(1)} %pad_clamp_fusion.8), kind=kCustom, calls=%fused_computation.clone.clone.1 | custom fusion | bytes 6144 | tf_op jit(solution)/shard_map/jit(searchsorted)/jit(_searchsorted_scan_impl)/vmap(jit(_searchsorted_scan_impl))/while/body/eval_jaxpr/gather | solution.py:14
  29.6 3.5 %gather_fusion = s32[512]{0:T(512)S(1)} fusion(s32[512]{0:T(512)S(1)} %get-tuple-element.276, u32[1024]{0:T(1024)S(1)} %pad_clamp_fusion.8), kind=kCustom, calls=%fused_computation.clone.clone.1 | custom fusion | bytes 6144 | tf_op jit(solution)/shard_map/jit(searchsorted)/jit(_searchsorted_scan_impl)/vmap(jit(_searchsorted_scan_impl))/while/body/eval_jaxpr/gather | solution.py:14
  56.0 6.9 %gather_fusion.3 = s32[1024]{0:T(1024)S(1)} fusion(s32[512]{0:T(512)S(1)} %get-tuple-element.197, s32[1024]{0:T(1024)S(1)} %fusion.4), kind=kCustom, calls=%fused_computation.3 | custom fusion | bytes 12288 | tf_op jit(solution)/shard_map/jit(_take)/gather | solution.py:37
  63.8 5.2 %all-to-all-start = ((s32[8,1,128]{2,1,0:T(1,128)}), s32[8,1,128]{2,1,0:T(1,128)S(1)}, u32[]{:S(2)}, u32[]{:S(2)}) async-start(s32[8,1,128]{2,1,0:T(1,128)} %reshape.227), calls=%async_computation | async-start | bytes 8192 | tf_op jit(solution)/shard_map/all_to_all | solution.py:49
  69.0 4.1 %gather_fusion.4 = bf16[1024,1024]{1,0:T(8,128)(2,1)S(1)} fusion(bf16[512,1024]{1,0:T(8,128)(2,1)S(1)} %copy-done, s32[1024]{0:T(1024)S(1)} %fusion.4), kind=kCustom, calls=%fused_computation.4 | custom fusion | bytes 4198400 | tf_op jit(solution)/shard_map/jit(_take)/gather | solution.py:34
  74.6 4.3 %all-to-all-start.2 = ((bf16[8,4,32,1024]{3,2,1,0:T(8,128)(2,1)}), bf16[8,4,32,1024]{3,2,1,0:T(8,128)(2,1)S(1)}, u32[]{:S(2)}, u32[]{:S(2)}) async-start(bf16[8,4,32,1024]{3,2,1,0:T(8,128)(2,1)} %broadcast_select_fusion.2), calls=%async_computation.2 | async-start | bytes 4194304 | tf_op jit(solution)/shard_map/all_to_all | solution.py:42
  83.6 18.6 %all-to-all-done.2 = bf16[8,4,32,1024]{3,2,1,0:T(8,128)(2,1)S(1)} async-done(((bf16[8,4,32,1024]{3,2,1,0:T(8,128)(2,1)}), bf16[8,4,32,1024]{3,2,1,0:T(8,128)(2,1)S(1)}, u32[]{:S(2)}, u32[]{:S(2)}) %all-to-all-start.2) | async-done | bytes 2097184 | tf_op jit(solution)/shard_map/all_to_all | solution.py:42
  102.1 4.6 %all-to-all-start.1 = ((s32[4,1,256]{2,1,0:T(1,128)}), s32[4,1,256]{2,1,0:T(1,128)S(1)}, u32[]{:S(2)}, u32[]{:S(2)}) async-start(s32[4,1,256]{2,1,0:T(1,128)} %reshape.229), calls=%async_computation.1 | async-start | bytes 8192 | tf_op jit(solution)/shard_map/all_to_all | solution.py:48
  111.1 3.6 %all-to-all-start.3 = ((bf16[8,4,32,1024]{3,2,0,1:T(8,128)(2,1)}), bf16[8,4,32,1024]{3,2,0,1:T(8,128)(2,1)S(1)}, u32[]{:S(2)}, u32[]{:S(2)}) async-start(bf16[8,4,32,1024]{3,2,0,1:T(8,128)(2,1)} %copy.24), calls=%async_computation.3 | async-start | bytes 4194304 | tf_op jit(solution)/shard_map/all_to_all | solution.py:41
  114.8 10.4 %while.51 = (s32[]{:T(128)}, u32[128]{0:T(128)S(1)}, u32[128]{0:T(128)S(1)}, s32[128]{0:T(128)S(1)}, s32[]{:T(128)}, /*index=5*/s32[]{:T(128)}, s32[]{}) while((s32[]{:T(128)}, u32[128]{0:T(128)S(1)}, u32[128]{0:T(128)S(1)}, s32[128]{0:T(128)S(1)}, s32[]{:T(128)}, /*index=5*/s32[]{:T(128)}, s32[]{}) %tuple.78), condition=%wide.region_9.10_spmd.clone, body=%wide.region_8.9_spmd.clone.sunk | while | flops 2692 | bytes 10852 | solution.py:14
  130.7 31.7 %all-to-all-done.3 = bf16[8,4,32,1024]{3,2,0,1:T(8,128)(2,1)S(1)} async-done(((bf16[8,4,32,1024]{3,2,0,1:T(8,128)(2,1)}), bf16[8,4,32,1024]{3,2,0,1:T(8,128)(2,1)S(1)}, u32[]{:S(2)}, u32[]{:S(2)}) %all-to-all-start.3) | async-done | bytes 2097184 | tf_op jit(solution)/shard_map/all_to_all | solution.py:41
  169.9 7.4 %all-to-all-start.4 = ((bf16[8,4,32,1024]{3,2,1,0:T(8,128)(2,1)}), bf16[8,4,32,1024]{3,2,1,0:T(8,128)(2,1)S(1)}, u32[]{:S(2)}, u32[]{:S(2)}) async-start(bf16[8,4,32,1024]{3,2,1,0:T(8,128)(2,1)} %bitcast.15), calls=%async_computation.4 | async-start | bytes 4194304 | tf_op jit(solution)/shard_map/all_to_all | solution.py:67
  181.3 19.2 %all-to-all-done.4 = bf16[8,4,32,1024]{3,2,1,0:T(8,128)(2,1)S(1)} async-done(((bf16[8,4,32,1024]{3,2,1,0:T(8,128)(2,1)}), bf16[8,4,32,1024]{3,2,1,0:T(8,128)(2,1)S(1)}, u32[]{:S(2)}, u32[]{:S(2)}) %all-to-all-start.4) | async-done | bytes 2097184 | tf_op jit(solution)/shard_map/all_to_all | solution.py:67
  200.5 4.1 %all-to-all-start.7 = ((bf16[4,64,1024]{2,1,0:T(8,128)(2,1)}), bf16[4,64,1024]{2,1,0:T(8,128)(2,1)}, u32[]{:S(2)}, u32[]{:S(2)}) async-start(bf16[4,64,1024]{2,1,0:T(8,128)(2,1)} %broadcast_select_fusion.3), calls=%async_computation.7 | async-start | bytes 1048576 | tf_op jit(solution)/shard_map/all_to_all | solution.py:92
  206.2 9.3 %all-to-all-done.7 = bf16[4,64,1024]{2,1,0:T(8,128)(2,1)} async-done(((bf16[4,64,1024]{2,1,0:T(8,128)(2,1)}), bf16[4,64,1024]{2,1,0:T(8,128)(2,1)}, u32[]{:S(2)}, u32[]{:S(2)}) %all-to-all-start.7) | async-done | bytes 524320 | tf_op jit(solution)/shard_map/all_to_all | solution.py:92
  215.6 4.9 %all-to-all-start.5 = ((bf16[8,4,32,1024]{3,2,0,1:T(8,128)(2,1)}), bf16[8,4,32,1024]{3,2,0,1:T(8,128)(2,1)}, u32[]{:S(2)}, u32[]{:S(2)}) async-start(bf16[8,4,32,1024]{3,2,0,1:T(8,128)(2,1)} %copy.26), calls=%async_computation.5 | async-start | bytes 4194304 | tf_op jit(solution)/shard_map/all_to_all | solution.py:66
  225.0 16.9 %psum.15 = bf16[1024]{0:T(1024)(128)(2,1)S(1)} all-reduce(bf16[1024]{0:T(1024)(128)(2,1)S(1)} %convert_reduce_fusion), channel_id=1, replica_groups=mesh['dp'=8,'cent'=4] {'dp'}, use_global_device_ids=true, to_apply=%region_14.15 | all-reduce | flops 1024 | bytes 4096 | tf_op jit(solution)/shard_map/psum | solution.py:104
  241.9 49.7 %all-reduce.2.cloned.1.call-done = bf16[1024,1024]{1,0:T(8,128)(2,1)} async-done(((bf16[1024,1024]{1,0:T(8,128)(2,1)}), bf16[1024,1024]{1,0:T(8,128)(2,1)}) %all-reduce.2.cloned.1.call-update) | async-done | bytes 2097168 | tf_op jit(solution)/shard_map/psum | solution.py:103
  291.6 3.7 %divide_convert_fusion = bf16[1024,1024]{1,0:T(8,128)(2,1)} fusion(bf16[1024,1024]{1,0:T(8,128)(2,1)} %all-reduce.2.cloned.1.call-done, f32[1024]{0:T(1024)S(1)} %convert_maximum_fusion), kind=kLoop, calls=%fused_computation.23 | loop fusion | flops 3145728 | bytes 4198400 | tf_op jit(solution)/shard_map/convert_element_type | solution.py:106
  (167 shorter events, 78.6 us)
Async XLA Ops:
  56.0 13.0 %copy-start = (bf16[512,1024]{1,0:T(8,128)(2,1)S(1)}, bf16[512,1024]{1,0:T(8,128)(2,1)}, u32[]{:S(2)}) copy-start(bf16[512,1024]{1,0:T(8,128)(2,1)} %param.7) | copy-start | bytes 3145732
  63.8 10.8 %all-to-all-start = ((s32[8,1,128]{2,1,0:T(1,128)}), s32[8,1,128]{2,1,0:T(1,128)S(1)}, u32[]{:S(2)}, u32[]{:S(2)}) async-start(s32[8,1,128]{2,1,0:T(1,128)} %reshape.227), calls=%async_computation | async-start | bytes 8192 | tf_op jit(solution)/shard_map/all_to_all | solution.py:49
  74.6 4.3 %copy-start.2 = (s32[128]{0:T(128)S(1)}, s32[128]{0:T(128)}, u32[]{:S(2)}) copy-start(s32[128]{0:T(128)} %param.9) | copy-start | bytes 1540
  74.6 27.5 %all-to-all-start.2 = ((bf16[8,4,32,1024]{3,2,1,0:T(8,128)(2,1)}), bf16[8,4,32,1024]{3,2,1,0:T(8,128)(2,1)S(1)}, u32[]{:S(2)}, u32[]{:S(2)}) async-start(bf16[8,4,32,1024]{3,2,1,0:T(8,128)(2,1)} %broadcast_select_fusion.2), calls=%async_computation.2 | async-start | bytes 4194304 | tf_op jit(solution)/shard_map/all_to_all | solution.py:42
  102.1 9.0 %all-to-all-start.1 = ((s32[4,1,256]{2,1,0:T(1,128)}), s32[4,1,256]{2,1,0:T(1,128)S(1)}, u32[]{:S(2)}, u32[]{:S(2)}) async-start(s32[4,1,256]{2,1,0:T(1,128)} %reshape.229), calls=%async_computation.1 | async-start | bytes 8192 | tf_op jit(solution)/shard_map/all_to_all | solution.py:48
  111.1 51.3 %all-to-all-start.3 = ((bf16[8,4,32,1024]{3,2,0,1:T(8,128)(2,1)}), bf16[8,4,32,1024]{3,2,0,1:T(8,128)(2,1)S(1)}, u32[]{:S(2)}, u32[]{:S(2)}) async-start(bf16[8,4,32,1024]{3,2,0,1:T(8,128)(2,1)} %copy.24), calls=%async_computation.3 | async-start | bytes 4194304 | tf_op jit(solution)/shard_map/all_to_all | solution.py:41
  162.4 7.5 %all-to-all-start.6 = ((s32[4,1,64]{2,1,0:T(1,128)}), s32[4,1,64]{2,1,0:T(1,128)S(1)}, u32[]{:S(2)}, u32[]{:S(2)}) async-start(s32[4,1,64]{2,1,0:T(1,128)} %select_n.129), calls=%async_computation.6 | async-start | bytes 4096 | tf_op jit(solution)/shard_map/all_to_all | solution.py:93
  166.3 11.1 %copy-start.1 = (bf16[128,1024]{1,0:T(8,128)(2,1)}, bf16[128,1024]{1,0:T(8,128)(2,1)S(1)}, u32[]{:S(2)}) copy-start(bf16[128,1024]{1,0:T(8,128)(2,1)S(1)} %fusion) | copy-start | bytes 786436
  169.9 30.6 %all-to-all-start.4 = ((bf16[8,4,32,1024]{3,2,1,0:T(8,128)(2,1)}), bf16[8,4,32,1024]{3,2,1,0:T(8,128)(2,1)S(1)}, u32[]{:S(2)}, u32[]{:S(2)}) async-start(bf16[8,4,32,1024]{3,2,1,0:T(8,128)(2,1)} %bitcast.15), calls=%async_computation.4 | async-start | bytes 4194304 | tf_op jit(solution)/shard_map/all_to_all | solution.py:67
  200.5 15.0 %all-to-all-start.7 = ((bf16[4,64,1024]{2,1,0:T(8,128)(2,1)}), bf16[4,64,1024]{2,1,0:T(8,128)(2,1)}, u32[]{:S(2)}, u32[]{:S(2)}) async-start(bf16[4,64,1024]{2,1,0:T(8,128)(2,1)} %broadcast_select_fusion.3), calls=%async_computation.7 | async-start | bytes 1048576 | tf_op jit(solution)/shard_map/all_to_all | solution.py:92
  215.6 79.7 %all-to-all-start.5 = ((bf16[8,4,32,1024]{3,2,0,1:T(8,128)(2,1)}), bf16[8,4,32,1024]{3,2,0,1:T(8,128)(2,1)}, u32[]{:S(2)}, u32[]{:S(2)}) async-start(bf16[8,4,32,1024]{3,2,0,1:T(8,128)(2,1)} %copy.26), calls=%async_computation.5 | async-start | bytes 4194304 | tf_op jit(solution)/shard_map/all_to_all | solution.py:66
  220.4 71.1 %all-reduce.2.cloned.1.call-start = ((), (), s32[]{:S(2)}) async-start(), calls=%async_computation.8 | async-start | bytes 4194304 | tf_op jit(solution)/shard_map/psum | solution.py:103
Sparse Core Ops, SparseCore 0:
  225.1 66.4 all-reduce.1
where the time goes:
time: 312 us; the launch traced here: 309 us
  waiting for transfers between devices  132 us (42%)
  local copies, waits for them, and re-layouts  82.6 us (26%)
  starting transfers between devices  37.4 us (12%)
  other arithmetic  19.8 us (6%)
  blocking collectives  16.9 us (5%)
  between operations  14.3 us (5%)
  matrix products  5.61 us (2%)
    psum x1, waiting for transfers between devices, body(): lax.psum(partial_value.astype(jnp.bfloat16), 'dp').astype(jnp.float32)  49.7 us
    gather x18, local copies, waits for them, and re-layouts, place_rows(): leading = jnp.searchsorted(sorted_targets, sorted_targets, side='left')  44.7 us
    all_to_all x1, waiting for transfers between devices, body(): lax.all_to_all(lax.all_to_all(send_rows, 'dp', split_axis=0, concat_axis=...  31.7 us
    all_to_all x1, waiting for transfers between devices, body(): lax.all_to_all(selected.astype(jnp.bfloat16).reshape(n_data, n_cent, capa...  19.2 us
    all_to_all x1, waiting for transfers between devices, body(): lax.all_to_all(send_rows, 'dp', split_axis=0, concat_axis=0, tiled=True)  18.6 us
    psum x1, blocking collectives, body(): lax.psum(tally.astype(jnp.bfloat16), 'dp').astype(jnp.float32)  16.9 us
    all_to_all x1, waiting for transfers between devices, body(): lax.all_to_all(send_fine, 'cent', split_axis=0, concat_axis=0, tiled=True)  9.32 us
    all_to_all x1, starting transfers between devices, body(): lax.all_to_all(selected.astype(jnp.bfloat16).reshape(n_data, n_cent, capa...  7.41 us
  transfers between devices with their start and end apart: 9, of which 7 were waited for; matrix products, arithmetic and copies ran while one was open for 15% of the time, Pallas kernels for 0%

commit v1 on v0

v1 whole, which is shorter than its diff:
```python
import functools

import jax
import jax.numpy as jnp
from jax import lax
from jax.experimental import pallas as pl
from jax.experimental.pallas import tpu as pltpu
from jax.sharding import PartitionSpec as P

COARSE = 4096
CHUNKS = 4
MESH = pl.DeviceIdType.MESH
F32 = jnp.float32
BF16 = jnp.bfloat16
I32 = jnp.int32


def log2(n):
    assert n & (n - 1) == 0
    return n.bit_length() - 1


def iota(shape, dim):
    return lax.broadcasted_iota(I32, shape, dim)


def to_col(row, rows):
    shape = (rows, row.shape[1])
    same = iota(shape, 0) == iota(shape, 1)
    return jnp.sum(jnp.where(same, row, 0.0), axis=1, keepdims=True)


def to_row(col, lanes):
    shape = (col.shape[0], lanes)
    same = iota(shape, 0) == iota(shape, 1)
    return jnp.sum(jnp.where(same, col, 0.0), axis=0, keepdims=True)


def kernel(cfg, *refs):
    (n_dp, n_cent, p_rows, fine, width, w, cap, cap2, block) = cfg
    (points, fa, ca, spread_out, fine_out, coarse_out,
     sel, send, recv, mt, m, pf, cz, gr, g,
     ids_s, ids_r, lab, glab, cnt_s, cnt_r, sp_s, sp_r, acc) = refs[:24]
    bits = log2(n_cent)
    rs_out = refs[24 : 24 + bits]
    rs_in = refs[24 + bits : 24 + 2 * bits]
    (a_ss, a_rs, rs_ss, rs_rs, ag_ss, ag_rs, g_ss, g_rs,
     id_ss, id_rs, lab_ss, lab_rs, cnt_ss, cnt_rs, gl_ss, gl_rs, sp_ss, sp_rs) = refs[24 + 2 * bits :]
    chunks = width // w
    group = n_cent * fine
    rows2 = n_cent * cap2
    lanes = max(cap, 128)
    me = lax.axis_index("dp")
    mz = lax.axis_index("cent")

    def reverse(z):
        return sum(((z // (1 << b)) % 2) * (1 << (bits - 1 - b)) for b in range(bits))

    place = reverse(mz)

    def at8(k):
        return pl.ds(pl.multiple_of(k * 8, 8), 8)

    def span(k, size):
        return pl.ds(pl.multiple_of(k * size, size), size)

    def dp_peer(j):
        return lax.rem(me + j, n_dp)

    def cent_peer(j):
        return lax.rem(mz + j, n_cent)

    started = []

    def copy(src, dst, ss, rs, d=None, z=None):
        made = pltpu.make_async_remote_copy(
            src_ref=src, dst_ref=dst, send_sem=ss, recv_sem=rs,
            device_id=(me if d is None else d, mz if z is None else z), device_id_type=MESH,
        )
        return made

    def go(*args, **kwargs):
        made = copy(*args, **kwargs)
        made.start()
        started.append(made)
        return made

    barrier = pltpu.get_barrier_semaphore()
    for j in range(1, n_dp):
        pl.semaphore_signal(barrier, inc=1, device_id=(dp_peer(j), mz), device_id_type=MESH)
    for j in range(1, n_cent):
        pl.semaphore_signal(barrier, inc=1, device_id=(me, cent_peer(j)), device_id_type=MESH)

    f_row = fa[...]
    d_row = (f_row >> log2(group)).astype(F32)
    z_row = (f_row & (group - 1)) >> log2(fine)
    p_row = (f_row & (fine - 1)) + sum(
        ((z_row >> b) & 1) << (bits - 1 - b + log2(fine)) for b in range(bits)
    )
    d_col = to_col(d_row, p_rows)
    p_col = to_col(p_row.astype(F32), p_rows)
    square = (p_rows, p_rows)
    earlier = jnp.logical_and(d_col == d_row, iota(square, 0) < iota(square, 1))
    rank_row = jnp.sum(jnp.where(earlier, 1.0, 0.0), axis=0, keepdims=True)
    rank_col = to_col(rank_row, p_rows)
    slot_row = d_row * cap + rank_row
    for k in range(n_dp):
        slots = (iota((cap, p_rows), 0) + k * cap).astype(F32)
        sel[pl.ds(k * cap, cap), :] = jnp.where(slots == slot_row, 1.0, 0.0).astype(BF16)

    pl.semaphore_wait(barrier, n_dp + n_cent - 2)

    lab[at8(place), :] = jnp.broadcast_to(ca[...], (8, fine))
    for j in range(1, n_cent):
        mine = lab.at[at8(place)]
        go(mine, mine, lab_ss.at[j], lab_rs.at[j], z=cent_peer(j))
    for c in range(chunks):
        moved = jnp.dot(sel[...], points[:, pl.ds(c * w, w)], preferred_element_type=F32)
        send[c] = moved.astype(BF16)
        for j in range(1, n_dp):
            go(send.at[c, span(dp_peer(j), cap)], recv.at[c, span(me, cap)],
               a_ss.at[c, j], a_rs.at[c, j], d=dp_peer(j))
        recv[c, span(me, cap), :] = send[c, span(me, cap), :]
        if c == 0:
            for k in range(n_dp):
                hit = jnp.where(d_col == k, rank_col, -1.0) == iota((p_rows, lanes), 1).astype(F32)
                row = jnp.sum(jnp.where(hit, p_col + 1.0, 0.0), axis=0, keepdims=True) - 1.0
                ids_s[pl.ds(k * 8, 8), :] = jnp.broadcast_to(row, (8, lanes))
            for j in range(1, n_dp):
                go(ids_s.at[at8(dp_peer(j))], ids_r.at[at8(me)], id_ss.at[j], id_rs.at[j], d=dp_peer(j))
            ids_r[at8(me), :] = ids_s[at8(me), :]

    for j in range(1, n_cent):
        copy(lab.at[at8(place)], lab.at[at8(reverse(cent_peer(n_cent - j)))],
             lab_ss.at[j], lab_rs.at[j], z=cent_peer(n_cent - j)).wait_recv()
    small = (fine, fine)
    before = iota(small, 0) < iota(small, 1)
    labels = jnp.zeros((1, rows2), F32)
    pick = []
    for k in range(n_cent):
        row = lab[pl.ds(k * 8, 1), :]
        inside = jnp.where((row >> log2(block)) == mz, 1.0, 0.0)
        inside_col = to_col(inside, fine)
        value_col = to_col((row & (block - 1)).astype(F32), fine)
        rank = jnp.sum(jnp.where(before, inside_col, 0.0), axis=0, keepdims=True)
        slot = jnp.where(inside > 0.0, rank + k * cap2, -1.0)
        slot_col = to_col(slot, fine)
        hit = slot_col == iota((fine, rows2), 1).astype(F32)
        labels = labels + jnp.sum(jnp.where(hit, value_col + 1.0, 0.0), axis=0, keepdims=True)
        pick.append(jnp.where(slot == iota((rows2, fine), 0).astype(F32), 1.0, 0.0).astype(BF16))
    glab[at8(me), :] = jnp.broadcast_to(labels - 1.0, (8, rows2))
    for j in range(1, n_dp):
        mine = glab.at[at8(me)]
        go(mine, mine, gl_ss.at[j], gl_rs.at[j], d=dp_peer(j))

    for j in range(1, n_dp):
        copy(ids_s.at[at8(me)], ids_r.at[at8(dp_peer(n_dp - j))],
             id_ss.at[j], id_rs.at[j], d=dp_peer(n_dp - j)).wait_recv()
    tally = jnp.zeros((1, group), F32)
    for k in range(n_dp):
        row = ids_r[pl.ds(k * 8, 1), :]
        col = to_col(row, cap)
        part = jnp.where(col == iota((cap, group), 1).astype(F32), 1.0, 0.0)
        mt[pl.ds(k * cap, cap), :] = part.astype(BF16)
        tally = tally + jnp.sum(part, axis=0, keepdims=True)
        if cap % 128 == 0:
            hit = row == iota((group, cap), 0).astype(F32)
            m[:, pl.ds(k * cap, cap)] = jnp.where(hit, 1.0, 0.0).astype(BF16)
    for k in range(n_cent):
        cnt_s[pl.ds(k * 8, 8), :] = jnp.broadcast_to(tally[:, k * fine : (k + 1) * fine], (8, fine))
    for j in range(1, n_cent):
        go(cnt_s.at[at8(reverse(cent_peer(j)))], cnt_r.at[pl.ds(j * 8, 8)],
           cnt_ss.at[j], cnt_rs.at[j], z=cent_peer(j))

    for j in range(1, n_dp):
        copy(glab.at[at8(me)], glab.at[at8(dp_peer(n_dp - j))],
             gl_ss.at[j], gl_rs.at[j], d=dp_peer(n_dp - j)).wait_recv()
    coarse_tally = jnp.zeros((block, 1), F32)
    for k in range(n_dp):
        row = glab[pl.ds(k * 8, 1), :]
        part = jnp.where(row == iota((block, rows2), 0).astype(F32), 1.0, 0.0)
        g[:, pl.ds(k * rows2, rows2)] = part.astype(BF16)
        coarse_tally = coarse_tally + jnp.sum(part, axis=1, keepdims=True)
    coarse_scale = jnp.maximum(coarse_tally, 1.0)

    for j in range(1, n_cent):
        copy(cnt_s.at[at8(place)], cnt_r.at[pl.ds(j * 8, 8)],
             cnt_ss.at[j], cnt_rs.at[j], z=cent_peer(n_cent - j)).wait_recv()
    total = cnt_s[at8(place), :]
    for j in range(1, n_cent):
        total = total + cnt_r[pl.ds(j * 8, 8), :]
    fine_scale = jnp.maximum(to_col(total[0:1, :], fine), 1.0)
    acc[...] = jnp.zeros_like(acc)

    def cent_partner(b):
        return mz + (1 - 2 * ((mz // (1 << b)) % 2)) * (1 << b)

    def keep(b):
        size = n_cent >> b
        return (place // size) * size

    def rs_parts(c, b):
        return (rs_out[b].at[c], rs_in[b].at[c], rs_ss.at[c, b], rs_rs.at[c, b])

    def rs_send(c, b):
        half = n_cent >> (b + 1)
        other = 2 * keep(b) + half - keep(b + 1)
        rs_out[b][c] = pf[c, pl.ds(pl.multiple_of(other * fine, fine), half * fine), :].astype(BF16)
        go(*rs_parts(c, b), z=cent_partner(b))

    def rs_add(c, b):
        half = n_cent >> (b + 1)
        copy(*rs_parts(c, b), z=cent_partner(b)).wait_recv()
        mine = pl.ds(pl.multiple_of(keep(b + 1) * fine, fine), half * fine)
        pf[c, mine, :] += rs_in[b][c].astype(F32)

    def ag_parts(c, b, sender_place):
        size = 1 << (bits - 1 - b)
        first = (sender_place // size) * size
        part = cz.at[c, pl.ds(pl.multiple_of(first * fine, fine), size * fine)]
        return (part, part, ag_ss.at[c, b], ag_rs.at[c, b])

    def ag_send(c, b):
        go(*ag_parts(c, b, place), z=cent_partner(b))

    def ag_wait(c, b):
        copy(*ag_parts(c, b, reverse(cent_partner(b))), z=cent_partner(b)).wait_recv()

    def sums(c):
        for j in range(1, n_dp):
            source = dp_peer(n_dp - j)
            copy(send.at[c, span(me, cap)], recv.at[c, span(source, cap)],
                 a_ss.at[c, j], a_rs.at[c, j], d=source).wait_recv()
        if cap % 128 == 0:
            pf[c] = jnp.dot(m[...], recv[c], preferred_element_type=F32)
        else:
            pf[c] = lax.dot_general(mt[...], recv[c], (((0,), (0,)), ((), ())),
                                    preferred_element_type=F32)
        rs_send(c, 0)

    def halve(b, c):
        rs_add(c, b - 1)
        rs_send(c, b)

    def centroids(c):
        rs_add(c, bits - 1)
        value = (pf[c, span(place, fine), :] / fine_scale).astype(BF16)
        cz[c, span(place, fine), :] = value
        fine_out[:, pl.ds(c * w, w)] = value
        ag_send(c, bits - 1)

    def double(b, c):
        ag_wait(c, b + 1)
        ag_send(c, b)

    def g_rows(c, d):
        return gr.at[c, span(d, rows2)]

    def g_args(c, k, d):
        return (g_rows(c, d), g_rows(c, d), g_ss.at[c, k], g_rs.at[c, k])

    if n_dp == 8:
        core = me % 2
        dx = (1 - 2 * ((me // 2) % 2)) * 2
        dy = (1 - 2 * ((me // 4) % 2)) * 4
        d1 = (1 - core) * dx + core * dy
        d2 = (1 - core) * dy + core * dx
        d3 = 1 - 2 * core

    def pick_rows(c):
        ag_wait(c, 0)
        mine = jnp.zeros((rows2, w), F32)
        for k in range(n_cent):
            mine = mine + jnp.dot(pick[k], cz[c, pl.ds(k * fine, fine), :], preferred_element_type=F32)
        gr[c, span(me, rows2), :] = mine.astype(BF16)
        if n_dp == 8:
            go(*g_args(c, 0, me), d=me + d1)
            go(*g_args(c, 1, me), d=me + d2)
            go(*g_args(c, 2, me), d=me + d3)
        else:
            for j in range(1, n_dp):
                go(*g_args(c, j, me), d=dp_peer(j))
        near = jnp.dot(mt[...], cz[c], preferred_element_type=F32)
        gap = jnp.square(recv[c].astype(F32) - near)
        acc[...] += sum(gap[:, i : i + 128] for i in range(0, w, 128))
        if c == chunks - 1:
            for k in range(n_dp):
                col = jnp.sum(acc[pl.ds(k * cap, cap), :], axis=1, keepdims=True) / width
                sp_s[pl.ds(k * 8, 8), :] = jnp.broadcast_to(to_row(col, lanes), (8, lanes))
            for j in range(1, n_dp):
                go(sp_s.at[at8(dp_peer(j))], sp_r.at[at8(me)], sp_ss.at[j], sp_rs.at[j], d=dp_peer(j))
            sp_r[at8(me), :] = sp_s[at8(me), :]

    def forward_one(c):
        if n_dp == 8:
            copy(*g_args(c, 0, me + d1), d=me + d1).wait_recv()
            go(*g_args(c, 3, me + d1), d=me + d2)
            go(*g_args(c, 4, me + d1), d=me + d3)
            copy(*g_args(c, 1, me + d2), d=me + d2).wait_recv()
            go(*g_args(c, 5, me + d2), d=me + d3)

    def forward_two(c):
        if n_dp == 8:
            copy(*g_args(c, 3, me + d1 + d2), d=me + d2).wait_recv()
            go(*g_args(c, 6, me + d1 + d2), d=me + d3)

    def finish(c):
        if n_dp == 8:
            copy(*g_args(c, 2, me + d3), d=me + d3).wait_recv()
            copy(*g_args(c, 4, me + d3 + d2), d=me + d3).wait_recv()
            copy(*g_args(c, 5, me + d3 + d1), d=me + d3).wait_recv()
            copy(*g_args(c, 6, me + d3 + d1 + d2), d=me + d3).wait_recv()
        else:
            for j in range(1, n_dp):
                source = dp_peer(n_dp - j)
                copy(*g_args(c, j, source), d=source).wait_recv()
        result = jnp.dot(g[...], gr[c], preferred_element_type=F32)
        coarse_out[:, pl.ds(c * w, w)] = (result / coarse_scale).astype(BF16)

    stages = [sums]
    stages += [functools.partial(halve, b) for b in range(1, bits)]
    stages += [centroids]
    stages += [functools.partial(double, b) for b in reversed(range(bits - 1))]
    stages += [pick_rows, forward_one, forward_two, finish]
    for tick in range(chunks + len(stages) - 1):
        for s in reversed(range(len(stages))):
            if 0 <= tick - s < chunks:
                stages[s](tick - s)

    for j in range(1, n_dp):
        source = dp_peer(n_dp - j)
        copy(sp_s.at[at8(me)], sp_r.at[at8(source)], sp_ss.at[j], sp_rs.at[j], d=source).wait_recv()
    spread = jnp.zeros((1, p_rows), F32)
    for k in range(n_dp):
        col = to_col(sp_r[pl.ds(k * 8, 1), :], cap)
        slots = (iota((cap, p_rows), 0) + k * cap).astype(F32)
        spread = spread + jnp.sum(jnp.where(slots == slot_row, col, 0.0), axis=0, keepdims=True)
    spread_out[...] = spread
    for made in started:
        made.wait_send()


def body(points, fine_assign, coarse_assign):
    n_dp = lax.axis_size("dp")
    n_cent = lax.axis_size("cent")
    p_rows, width = points.shape
    fine = coarse_assign.shape[0]
    sources = n_dp * n_cent
    cap = max(2, 2 * p_rows // sources) * n_cent
    cap2 = max(2, 2 * fine // n_cent)
    block = COARSE // n_cent
    w = width // CHUNKS
    bits = log2(n_cent)
    group, slots, rows2, lanes = n_cent * fine, n_dp * cap, n_cent * cap2, max(cap, 128)
    cfg = (n_dp, n_cent, p_rows, fine, width, w, cap, cap2, block)
    halves = [pltpu.VMEM((CHUNKS, (n_cent >> (b + 1)) * fine, w), BF16) for b in range(bits)]
    dma = pltpu.SemaphoreType.DMA
    scratch = [
        pltpu.VMEM((slots, p_rows), BF16),
        pltpu.VMEM((CHUNKS, slots, w), BF16),
        pltpu.VMEM((CHUNKS, slots, w), BF16),
        pltpu.VMEM((slots, group), BF16),
        pltpu.VMEM((group, slots) if cap % 128 == 0 else (16, 128), BF16),
        pltpu.VMEM((CHUNKS, group, w), F32),
        pltpu.VMEM((CHUNKS, group, w), BF16),
        pltpu.VMEM((CHUNKS, n_dp * rows2, w), BF16),
        pltpu.VMEM((block, n_dp * rows2), BF16),
        pltpu.VMEM((n_dp * 8, lanes), F32),
        pltpu.VMEM((n_dp * 8, lanes), F32),
        pltpu.VMEM((n_cent * 8, fine), I32),
        pltpu.VMEM((n_dp * 8, rows2), F32),
        pltpu.VMEM((n_cent * 8, fine), F32),
        pltpu.VMEM((n_cent * 8, fine), F32),
        pltpu.VMEM((n_dp * 8, lanes), F32),
        pltpu.VMEM((n_dp * 8, lanes), F32),
        pltpu.VMEM((slots, 128), F32),
        *halves,
        *halves,
        dma((CHUNKS, n_dp)), dma((CHUNKS, n_dp)),
        dma((CHUNKS, bits)), dma((CHUNKS, bits)),
        dma((CHUNKS, bits)), dma((CHUNKS, bits)),
        dma((CHUNKS, n_dp)), dma((CHUNKS, n_dp)),
        dma((n_dp,)), dma((n_dp,)),
        dma((n_cent,)), dma((n_cent,)),
        dma((n_cent,)), dma((n_cent,)),
        dma((n_dp,)), dma((n_dp,)),
        dma((n_dp,)), dma((n_dp,)),
    ]
    vmem = pl.BlockSpec(memory_space=pltpu.VMEM)
    spread, fine_centroids, coarse_centroids = pl.pallas_call(
        functools.partial(kernel, cfg),
        out_shape=(
            jax.ShapeDtypeStruct((1, p_rows), F32),
            jax.ShapeDtypeStruct((fine, width), BF16),
            jax.ShapeDtypeStruct((block, width), BF16),
        ),
        in_specs=[vmem] * 3,
        out_specs=(vmem,) * 3,
        scratch_shapes=scratch,
        compiler_params=pltpu.CompilerParams(
            collective_id=0, has_side_effects=True, vmem_limit_bytes=60 * 1024 * 1024
        ),
        cost_estimate=pl.CostEstimate(
            flops=2 * width * (slots * (p_rows + 2 * group) + block * n_dp * rows2),
            bytes_accessed=2 * width * (p_rows + fine + block),
            transcendentals=0,
        ),
    )(points, fine_assign.reshape(1, p_rows), coarse_assign.reshape(1, fine))
    return (spread.reshape(p_rows), fine_centroids, coarse_centroids)


def solution(mesh):
    placed = (P(("dp", "cent"), None), P(("dp", "cent")), P(("dp", "cent")))
    return jax.shard_map(
        body,
        mesh=mesh,
        in_specs=placed,
        out_specs=(P(("dp", "cent")), P(("dp", "cent"), None), P("cent", None)),
        check_vma=False,
    )
```

time: 312 us -> 101 us (0.32)
  waiting for transfers between devices: 132 us -> 0 us
  Pallas kernels: 0 us -> 94.3 us
  local copies, waits for them, and re-layouts: 82.6 us -> 6 us
  starting transfers between devices: 37.4 us -> 0 us
  other arithmetic: 19.8 us -> 0 us
  blocking collectives: 16.9 us -> 0 us
  between operations: 14.3 us -> 0.64 us
  matrix products: 5.61 us -> 0 us
    pallas_call x0 -> x1, Pallas kernels: none -> 94.3 us  [body(): pl.pallas_call(functools.partial(kernel, cfg), out_shape=(jax.ShapeDtypeS...]
    all_to_all x8 -> x0, waiting for transfers between devices: 82 us -> none  [the longest x1 31.7 us: body(): lax.all_to_all(lax.all_to_all(send_rows, 'dp', split_axis=0, concat_axis=...]
    gather x26 -> x0, local copies, waits for them, and re-layouts: 67.1 us -> none  [the longest x18 44.7 us: place_rows(): leading = jnp.searchsorted(sorted_targets, sorted_targets, side='left')]
    psum x1 -> x0, waiting for transfers between devices: 49.7 us -> none  [body(): lax.psum(partial_value.astype(jnp.bfloat16), 'dp').astype(jnp.float32)]
    all_to_all x8 -> x0, starting transfers between devices: 37.4 us -> none  [the longest x1 7.41 us: body(): lax.all_to_all(selected.astype(jnp.bfloat16).reshape(n_data, n_cent, capa...]
    psum x1 -> x0, blocking collectives: 16.9 us -> none  [body(): lax.psum(tally.astype(jnp.bfloat16), 'dp').astype(jnp.float32)]
    scatter x4 -> x0, local copies, waits for them, and re-layouts: 6.83 us -> none  [the longest x2 3.42 us: place_rows(): slot_source = jnp.full((total_slots,), count, jnp.int32).at[destination]....]
    sort x2 -> x0, other arithmetic: 6.3 us -> none  [place_rows(): ranking = jnp.argsort(targets, stable=True)]
  transfers between devices with their start and end apart: 9 -> 0, of which waited for: 7 -> 0; matrix products, arithmetic and copies ran while one was open for 15% -> 0% of each run, Pallas kernels for 0% -> 0%
where the time goes in v1:
time: 101 us
  Pallas kernels  94.3 us (93%)
  local copies, waits for them, and re-layouts  6 us (6%)
    pallas_call x1, Pallas kernels, body(): pl.pallas_call(functools.partial(kernel, cfg), out_shape=(jax.ShapeDtypeS...  94.3 us
    unnamed x3, local copies, waits for them, and re-layouts  6 us

profile of v1, /device:TPU:1, one launch (start us, length us, event | category | flops | bytes accessed | tf_op | source)
XLA Modules:
  0.0 100.9 jit_solution(17457124732531474795)
XLA Ops:
  0.6 94.3 %shard_map.58 = (f32[1,512]{1,0:T(1,128)}, bf16[128,1024]{1,0:T(8,128)(2,1)}, bf16[1024,1024]{1,0:T(8,128)(2,1)}) custom-call(bf16[512,1024]{1,0:T(8,128)(2,1)} %refs_0_.1, s32[1,512]{1,0:T(1,128)} %bitcast.4, s32[1,128]{1,0:T(1,128)} %bitcast.5), custom_call_target="tpu_custom_call" | custom-call | flops 7516192768 | bytes 3407872 | tf_op jit(solution)/shard_map/pallas_call | solution.py:390
  94.9 1.2 %copy.9 = f32[512]{0:T(512)} copy(f32[512]{0:T(512)} %bitcast.3) | data formatting | bytes 4096
  96.2 1.7 %copy.10 = bf16[128,1024]{1,0:T(8,128)(2,1)} copy(bf16[128,1024]{1,0:T(8,128)(2,1)} %get-tuple-element.13) | data formatting | bytes 524288
  97.9 3.1 %copy.11 = bf16[1024,1024]{1,0:T(8,128)(2,1)} copy(bf16[1024,1024]{1,0:T(8,128)(2,1)} %get-tuple-element.14) | data formatting | bytes 4194304

commit v2 on v1

--- a/solution.py
+++ b/solution.py
@@ -98,11 +98,9 @@
         ((z_row >> b) & 1) << (bits - 1 - b + log2(fine)) for b in range(bits)
     )
     d_col = to_col(d_row, p_rows)
-    p_col = to_col(p_row.astype(F32), p_rows)
     square = (p_rows, p_rows)
     earlier = jnp.logical_and(d_col == d_row, iota(square, 0) < iota(square, 1))
     rank_row = jnp.sum(jnp.where(earlier, 1.0, 0.0), axis=0, keepdims=True)
-    rank_col = to_col(rank_row, p_rows)
     slot_row = d_row * cap + rank_row
     for k in range(n_dp):
         slots = (iota((cap, p_rows), 0) + k * cap).astype(F32)
@@ -114,21 +112,31 @@
     for j in range(1, n_cent):
         mine = lab.at[at8(place)]
         go(mine, mine, lab_ss.at[j], lab_rs.at[j], z=cent_peer(j))
-    for c in range(chunks):
+    def prepare(c):
         moved = jnp.dot(sel[...], points[:, pl.ds(c * w, w)], preferred_element_type=F32)
         send[c] = moved.astype(BF16)
+        recv[c, span(me, cap), :] = send[c, span(me, cap), :]
+
+    def dispatch(c):
         for j in range(1, n_dp):
             go(send.at[c, span(dp_peer(j), cap)], recv.at[c, span(me, cap)],
                a_ss.at[c, j], a_rs.at[c, j], d=dp_peer(j))
-        recv[c, span(me, cap), :] = send[c, span(me, cap), :]
-        if c == 0:
-            for k in range(n_dp):
-                hit = jnp.where(d_col == k, rank_col, -1.0) == iota((p_rows, lanes), 1).astype(F32)
-                row = jnp.sum(jnp.where(hit, p_col + 1.0, 0.0), axis=0, keepdims=True) - 1.0
-                ids_s[pl.ds(k * 8, 8), :] = jnp.broadcast_to(row, (8, lanes))
-            for j in range(1, n_dp):
-                go(ids_s.at[at8(dp_peer(j))], ids_r.at[at8(me)], id_ss.at[j], id_rs.at[j], d=dp_peer(j))
-            ids_r[at8(me), :] = ids_s[at8(me), :]
+
+    prepare(0)
+    dispatch(0)
+    p_col = to_col(p_row.astype(F32), p_rows)
+    rank_col = to_col(rank_row, p_rows)
+    for k in range(n_dp):
+        hit = jnp.where(d_col == k, rank_col, -1.0) == iota((p_rows, lanes), 1).astype(F32)
+        row = jnp.sum(jnp.where(hit, p_col + 1.0, 0.0), axis=0, keepdims=True) - 1.0
+        ids_s[pl.ds(k * 8, 8), :] = jnp.broadcast_to(row, (8, lanes))
+    for j in range(1, n_dp):
+        go(ids_s.at[at8(dp_peer(j))], ids_r.at[at8(me)], id_ss.at[j], id_rs.at[j], d=dp_peer(j))
+    ids_r[at8(me), :] = ids_s[at8(me), :]
+    for c in range(1, chunks):
+        prepare(c)
+        if c == 1:
+            dispatch(1)
 
     for j in range(1, n_cent):
         copy(lab.at[at8(place)], lab.at[at8(reverse(cent_peer(n_cent - j)))],
@@ -214,23 +222,24 @@
         mine = pl.ds(pl.multiple_of(keep(b + 1) * fine, fine), half * fine)
         pf[c, mine, :] += rs_in[b][c].astype(F32)
 
-    def ag_parts(c, b, sender_place):
-        size = 1 << (bits - 1 - b)
-        first = (sender_place // size) * size
-        part = cz.at[c, pl.ds(pl.multiple_of(first * fine, fine), size * fine)]
-        return (part, part, ag_ss.at[c, b], ag_rs.at[c, b])
-
-    def ag_send(c, b):
-        go(*ag_parts(c, b, place), z=cent_partner(b))
-
-    def ag_wait(c, b):
-        copy(*ag_parts(c, b, reverse(cent_partner(b))), z=cent_partner(b)).wait_recv()
+    def ag_send(c):
+        mine = cz.at[c, span(place, fine)]
+        for j in range(1, n_cent):
+            go(mine, mine, ag_ss.at[c, j], ag_rs.at[c, j], z=cent_peer(j))
+
+    def ag_wait(c):
+        for j in range(1, n_cent):
+            source = cent_peer(n_cent - j)
+            theirs = cz.at[c, span(reverse(source), fine)]
+            copy(theirs, theirs, ag_ss.at[c, j], ag_rs.at[c, j], z=source).wait_recv()
 
     def sums(c):
         for j in range(1, n_dp):
             source = dp_peer(n_dp - j)
             copy(send.at[c, span(me, cap)], recv.at[c, span(source, cap)],
                  a_ss.at[c, j], a_rs.at[c, j], d=source).wait_recv()
+        if c + 2 < chunks:
+            dispatch(c + 2)
         if cap % 128 == 0:
             pf[c] = jnp.dot(m[...], recv[c], preferred_element_type=F32)
         else:
@@ -247,11 +256,7 @@
         value = (pf[c, span(place, fine), :] / fine_scale).astype(BF16)
         cz[c, span(place, fine), :] = value
         fine_out[:, pl.ds(c * w, w)] = value
-        ag_send(c, bits - 1)
-
-    def double(b, c):
-        ag_wait(c, b + 1)
-        ag_send(c, b)
+        ag_send(c)
 
     def g_rows(c, d):
         return gr.at[c, span(d, rows2)]
@@ -268,7 +273,7 @@
         d3 = 1 - 2 * core
 
     def pick_rows(c):
-        ag_wait(c, 0)
+        ag_wait(c)
         mine = jnp.zeros((rows2, w), F32)
         for k in range(n_cent):
             mine = mine + jnp.dot(pick[k], cz[c, pl.ds(k * fine, fine), :], preferred_element_type=F32)
@@ -320,7 +325,6 @@
     stages = [sums]
     stages += [functools.partial(halve, b) for b in range(1, bits)]
     stages += [centroids]
-    stages += [functools.partial(double, b) for b in reversed(range(bits - 1))]
     stages += [pick_rows, forward_one, forward_two, finish]
     for tick in range(chunks + len(stages) - 1):
         for s in reversed(range(len(stages))):
@@ -338,6 +342,15 @@
     spread_out[...] = spread
     for made in started:
         made.wait_send()
+
+
+def place_results(*refs):
+    n = (len(refs) - 1) // 2
+    moves = [pltpu.make_async_copy(refs[i], refs[n + i], refs[-1].at[i]) for i in range(n)]
+    for move in moves:
+        move.start()
+    for move in moves:
+        move.wait()
 
 
 def body(points, fine_assign, coarse_assign):
@@ -378,7 +391,7 @@
         *halves,
         dma((CHUNKS, n_dp)), dma((CHUNKS, n_dp)),
         dma((CHUNKS, bits)), dma((CHUNKS, bits)),
-        dma((CHUNKS, bits)), dma((CHUNKS, bits)),
+        dma((CHUNKS, n_cent)), dma((CHUNKS, n_cent)),
         dma((CHUNKS, n_dp)), dma((CHUNKS, n_dp)),
         dma((n_dp,)), dma((n_dp,)),
         dma((n_cent,)), dma((n_cent,)),
@@ -387,7 +400,7 @@
         dma((n_dp,)), dma((n_dp,)),
     ]
     vmem = pl.BlockSpec(memory_space=pltpu.VMEM)
-    spread, fine_centroids, coarse_centroids = pl.pallas_call(
+    results = pl.pallas_call(
         functools.partial(kernel, cfg),
         out_shape=(
             jax.ShapeDtypeStruct((1, p_rows), F32),
@@ -406,6 +419,14 @@
             transcendentals=0,
         ),
     )(points, fine_assign.reshape(1, p_rows), coarse_assign.reshape(1, fine))
+    anywhere = pl.BlockSpec(memory_space=pl.ANY)
+    spread, fine_centroids, coarse_centroids = pl.pallas_call(
+        place_results,
+        out_shape=tuple(jax.ShapeDtypeStruct(r.shape, r.dtype) for r in results),
+        in_specs=[anywhere] * 3,
+        out_specs=(anywhere,) * 3,
+        scratch_shapes=[dma((3,))],
+    )(*results)
     return (spread.reshape(p_rows), fine_centroids, coarse_centroids)
 
 

time: 101 us -> 156 us (1.54)
  Pallas kernels: 94.3 us -> 155 us
  local copies, waits for them, and re-layouts: 6 us -> 0 us
    pallas_call x0 -> x1, Pallas kernels: none -> 72.7 us  [body(): pl.pallas_call(place_results, out_shape=tuple((jax.ShapeDtypeStruct(r.sha...]
    pallas_call x1, Pallas kernels: 94.3 us -> 82.6 us  [body(): pl.pallas_call(functools.partial(kernel, cfg), out_shape=(jax.ShapeDtypeS...]
    unnamed x3 -> x0, local copies, waits for them, and re-layouts: 6 us -> none
where the time goes in v2:
time: 156 us
  Pallas kernels  155 us (99%)
    pallas_call x1, Pallas kernels, body(): pl.pallas_call(functools.partial(kernel, cfg), out_shape=(jax.ShapeDtypeS...  82.6 us
    pallas_call x1, Pallas kernels, body(): pl.pallas_call(place_results, out_shape=tuple((jax.ShapeDtypeStruct(r.sha...  72.7 us

profile of v2, /device:TPU:1, one launch (start us, length us, event | category | flops | bytes accessed | tf_op | source)
XLA Modules:
  0.0 155.9 jit_solution(16762715308737483725)
XLA Ops:
  0.6 82.6 %shard_map.58 = (f32[1,512]{1,0:T(1,128)}, bf16[128,1024]{1,0:T(8,128)(2,1)}, bf16[1024,1024]{1,0:T(8,128)(2,1)}) custom-call(bf16[512,1024]{1,0:T(8,128)(2,1)} %refs_0_.1, s32[1,512]{1,0:T(1,128)} %bitcast.3, s32[1,128]{1,0:T(1,128)} %bitcast.5), custom_call_target="tpu_custom_call" | custom-call | flops 7516192768 | bytes 3407872 | tf_op jit(solution)/shard_map/pallas_call | solution.py:403
  83.3 72.7 %shard_map.59 = (f32[1,512]{1,0:T(1,128)}, bf16[128,1024]{1,0:T(8,128)(2,1)}, bf16[1024,1024]{1,0:T(8,128)(2,1)}) custom-call(f32[1,512]{1,0:T(1,128)} %get-tuple-element.9.refs_0_, bf16[128,1024]{1,0:T(8,128)(2,1)} %get-tuple-element.10.refs_1_, bf16[1024,1024]{1,0:T(8,128)(2,1)} %get-tuple-element.11.refs_2_), custom_call_target="tpu_custom_call" | custom-call | tf_op jit(solution)/shard_map/pallas_call | solution.py:423

commit v3 on v2

--- a/solution.py
+++ b/solution.py
@@ -8,7 +8,9 @@
 from jax.sharding import PartitionSpec as P
 
 COARSE = 4096
-CHUNKS = 4
+CHUNKS = 8
+AHEAD = 3
+PARTS = 4
 MESH = pl.DeviceIdType.MESH
 F32 = jnp.float32
 BF16 = jnp.bfloat16
@@ -48,6 +50,7 @@
      id_ss, id_rs, lab_ss, lab_rs, cnt_ss, cnt_rs, gl_ss, gl_rs, sp_ss, sp_rs) = refs[24 + 2 * bits :]
     chunks = width // w
     group = n_cent * fine
+    live = bits + 1
     rows2 = n_cent * cap2
     lanes = max(cap, 128)
     me = lax.axis_index("dp")
@@ -135,8 +138,8 @@
     ids_r[at8(me), :] = ids_s[at8(me), :]
     for c in range(1, chunks):
         prepare(c)
-        if c == 1:
-            dispatch(1)
+        if c < AHEAD:
+            dispatch(c)
 
     for j in range(1, n_cent):
         copy(lab.at[at8(place)], lab.at[at8(reverse(cent_peer(n_cent - j)))],
@@ -180,25 +183,30 @@
         go(cnt_s.at[at8(reverse(cent_peer(j)))], cnt_r.at[pl.ds(j * 8, 8)],
            cnt_ss.at[j], cnt_rs.at[j], z=cent_peer(j))
 
-    for j in range(1, n_dp):
-        copy(glab.at[at8(me)], glab.at[at8(dp_peer(n_dp - j))],
-             gl_ss.at[j], gl_rs.at[j], d=dp_peer(n_dp - j)).wait_recv()
-    coarse_tally = jnp.zeros((block, 1), F32)
-    for k in range(n_dp):
-        row = glab[pl.ds(k * 8, 1), :]
-        part = jnp.where(row == iota((block, rows2), 0).astype(F32), 1.0, 0.0)
-        g[:, pl.ds(k * rows2, rows2)] = part.astype(BF16)
-        coarse_tally = coarse_tally + jnp.sum(part, axis=1, keepdims=True)
-    coarse_scale = jnp.maximum(coarse_tally, 1.0)
-
-    for j in range(1, n_cent):
-        copy(cnt_s.at[at8(place)], cnt_r.at[pl.ds(j * 8, 8)],
-             cnt_ss.at[j], cnt_rs.at[j], z=cent_peer(n_cent - j)).wait_recv()
-    total = cnt_s[at8(place), :]
-    for j in range(1, n_cent):
-        total = total + cnt_r[pl.ds(j * 8, 8), :]
-    fine_scale = jnp.maximum(to_col(total[0:1, :], fine), 1.0)
     acc[...] = jnp.zeros_like(acc)
+
+    def fine_counts():
+        for j in range(1, n_cent):
+            copy(cnt_s.at[at8(place)], cnt_r.at[pl.ds(j * 8, 8)],
+                 cnt_ss.at[j], cnt_rs.at[j], z=cent_peer(n_cent - j)).wait_recv()
+        total = cnt_s[at8(place), :]
+        for j in range(1, n_cent):
+            total = total + cnt_r[pl.ds(j * 8, 8), :]
+        fine_scale = jnp.maximum(to_col(total[0:1, :], fine), 1.0)
+        return fine_scale
+
+    def coarse_members():
+        for j in range(1, n_dp):
+            copy(glab.at[at8(me)], glab.at[at8(dp_peer(n_dp - j))],
+                 gl_ss.at[j], gl_rs.at[j], d=dp_peer(n_dp - j)).wait_recv()
+        coarse_tally = jnp.zeros((block, 1), F32)
+        for k in range(n_dp):
+            row = glab[pl.ds(k * 8, 1), :]
+            part = jnp.where(row == iota((block, rows2), 0).astype(F32), 1.0, 0.0)
+            g[:, pl.ds(k * rows2, rows2)] = part.astype(BF16)
+            coarse_tally = coarse_tally + jnp.sum(part, axis=1, keepdims=True)
+        coarse_scale = jnp.maximum(coarse_tally, 1.0)
+        return coarse_scale
 
     def cent_partner(b):
         return mz + (1 - 2 * ((mz // (1 << b)) % 2)) * (1 << b)
@@ -213,14 +221,14 @@
     def rs_send(c, b):
         half = n_cent >> (b + 1)
         other = 2 * keep(b) + half - keep(b + 1)
-        rs_out[b][c] = pf[c, pl.ds(pl.multiple_of(other * fine, fine), half * fine), :].astype(BF16)
+        rs_out[b][c] = pf[c % live, pl.ds(pl.multiple_of(other * fine, fine), half * fine), :].astype(BF16)
         go(*rs_parts(c, b), z=cent_partner(b))
 
     def rs_add(c, b):
         half = n_cent >> (b + 1)
         copy(*rs_parts(c, b), z=cent_partner(b)).wait_recv()
         mine = pl.ds(pl.multiple_of(keep(b + 1) * fine, fine), half * fine)
-        pf[c, mine, :] += rs_in[b][c].astype(F32)
+        pf[c % live, mine, :] += rs_in[b][c].astype(F32)
 
     def ag_send(c):
         mine = cz.at[c, span(place, fine)]
@@ -238,12 +246,12 @@
             source = dp_peer(n_dp - j)
             copy(send.at[c, span(me, cap)], recv.at[c, span(source, cap)],
                  a_ss.at[c, j], a_rs.at[c, j], d=source).wait_recv()
-        if c + 2 < chunks:
-            dispatch(c + 2)
+        if c + AHEAD < chunks:
+            dispatch(c + AHEAD)
         if cap % 128 == 0:
-            pf[c] = jnp.dot(m[...], recv[c], preferred_element_type=F32)
+            pf[c % live] = jnp.dot(m[...], recv[c], preferred_element_type=F32)
         else:
-            pf[c] = lax.dot_general(mt[...], recv[c], (((0,), (0,)), ((), ())),
+            pf[c % live] = lax.dot_general(mt[...], recv[c], (((0,), (0,)), ((), ())),
                                     preferred_element_type=F32)
         rs_send(c, 0)
 
@@ -253,7 +261,7 @@
 
     def centroids(c):
         rs_add(c, bits - 1)
-        value = (pf[c, span(place, fine), :] / fine_scale).astype(BF16)
+        value = (pf[c % live, span(place, fine), :] / fine_scale).astype(BF16)
         cz[c, span(place, fine), :] = value
         fine_out[:, pl.ds(c * w, w)] = value
         ag_send(c)
@@ -330,6 +338,10 @@
         for s in reversed(range(len(stages))):
             if 0 <= tick - s < chunks:
                 stages[s](tick - s)
+        if tick == 0:
+            fine_scale = fine_counts()
+        if tick == 1:
+            coarse_scale = coarse_members()
 
     for j in range(1, n_dp):
         source = dp_peer(n_dp - j)
@@ -345,11 +357,27 @@
 
 
 def place_results(*refs):
-    n = (len(refs) - 1) // 2
-    moves = [pltpu.make_async_copy(refs[i], refs[n + i], refs[-1].at[i]) for i in range(n)]
-    for move in moves:
+    n = 3
+    ins, outs, held, (sem_in, sem_out) = refs[:n], refs[n : 2 * n], refs[2 * n : 3 * n], refs[3 * n :]
+    parts = []
+    for i in (2, 1, 0):
+        count = PARTS if i == 2 else 1
+        rows = ins[i].shape[0] // count
+        parts += [(i, pl.ds(k * rows, rows)) for k in range(count)]
+    first = [
+        pltpu.make_async_copy(ins[i].at[at], held[i].at[at], sem_in.at[k])
+        for k, (i, at) in enumerate(parts)
+    ]
+    second = [
+        pltpu.make_async_copy(held[i].at[at], outs[i].at[at], sem_out.at[k])
+        for k, (i, at) in enumerate(parts)
+    ]
+    for move in first:
         move.start()
-    for move in moves:
+    for k, move in enumerate(first):
+        move.wait()
+        second[k].start()
+    for move in second:
         move.wait()
 
 
@@ -374,7 +402,7 @@
         pltpu.VMEM((CHUNKS, slots, w), BF16),
         pltpu.VMEM((slots, group), BF16),
         pltpu.VMEM((group, slots) if cap % 128 == 0 else (16, 128), BF16),
-        pltpu.VMEM((CHUNKS, group, w), F32),
+        pltpu.VMEM((bits + 1, group, w), F32),
         pltpu.VMEM((CHUNKS, group, w), BF16),
         pltpu.VMEM((CHUNKS, n_dp * rows2, w), BF16),
         pltpu.VMEM((block, n_dp * rows2), BF16),
@@ -425,7 +453,11 @@
         out_shape=tuple(jax.ShapeDtypeStruct(r.shape, r.dtype) for r in results),
         in_specs=[anywhere] * 3,
         out_specs=(anywhere,) * 3,
-        scratch_shapes=[dma((3,))],
+        scratch_shapes=[
+            *(pltpu.VMEM(r.shape, r.dtype) for r in results),
+            dma((PARTS + 2,)),
+            dma((PARTS + 2,)),
+        ],
     )(*results)
     return (spread.reshape(p_rows), fine_centroids, coarse_centroids)
 

time: 156 us -> 84 us (0.54)
  Pallas kernels: 155 us -> 83 us
    pallas_call x1, Pallas kernels: 72.7 us -> 2.54 us  [body(): pl.pallas_call(place_results, out_shape=tuple((jax.ShapeDtypeStruct(r.sha...]
    pallas_call x1, Pallas kernels: 82.6 us -> 80.5 us  [body(): pl.pallas_call(functools.partial(kernel, cfg), out_shape=(jax.ShapeDtypeS...]
where the time goes in v3:
time: 84 us; the launch traced here: 83.8 us
  Pallas kernels  83 us (99%)
    pallas_call x1, Pallas kernels, body(): pl.pallas_call(functools.partial(kernel, cfg), out_shape=(jax.ShapeDtypeS...  80.5 us
    pallas_call x1, Pallas kernels, body(): pl.pallas_call(place_results, out_shape=tuple((jax.ShapeDtypeStruct(r.sha...  2.54 us

profile of v3, /device:TPU:1, one launch (start us, length us, event | category | flops | bytes accessed | tf_op | source)
XLA Modules:
  0.0 83.8 jit_solution(16400184017952024596)
XLA Ops:
  0.6 80.5 %shard_map.58 = (f32[1,512]{1,0:T(1,128)}, bf16[128,1024]{1,0:T(8,128)(2,1)}, bf16[1024,1024]{1,0:T(8,128)(2,1)}) custom-call(bf16[512,1024]{1,0:T(8,128)(2,1)} %refs_0_.1, s32[1,512]{1,0:T(1,128)} %bitcast.3, s32[1,128]{1,0:T(1,128)} %bitcast.5), custom_call_target="tpu_custom_call" | custom-call | flops 7516192768 | bytes 3407872 | tf_op jit(solution)/shard_map/pallas_call | solution.py:431
  81.1 2.5 %shard_map.59 = (f32[1,512]{1,0:T(1,128)}, bf16[128,1024]{1,0:T(8,128)(2,1)}, bf16[1024,1024]{1,0:T(8,128)(2,1)}) custom-call(f32[1,512]{1,0:T(1,128)} %get-tuple-element.9.refs_0_, bf16[128,1024]{1,0:T(8,128)(2,1)} %get-tuple-element.10.refs_1_, bf16[1024,1024]{1,0:T(8,128)(2,1)} %get-tuple-element.11.refs_2_), custom_call_target="tpu_custom_call" | custom-call | tf_op jit(solution)/shard_map/pallas_call | solution.py:451

commit v4 on v3

--- a/solution.py
+++ b/solution.py
@@ -8,8 +8,7 @@
 from jax.sharding import PartitionSpec as P
 
 COARSE = 4096
-CHUNKS = 8
-AHEAD = 3
+AHEAD = 4
 PARTS = 4
 MESH = pl.DeviceIdType.MESH
 F32 = jnp.float32
@@ -39,16 +38,18 @@
 
 
 def kernel(cfg, *refs):
-    (n_dp, n_cent, p_rows, fine, width, w, cap, cap2, block) = cfg
+    (n_dp, n_cent, p_rows, fine, width, widths, cap, cap2, block) = cfg
     (points, fa, ca, spread_out, fine_out, coarse_out,
-     sel, send, recv, mt, m, pf, cz, gr, g,
-     ids_s, ids_r, lab, glab, cnt_s, cnt_r, sp_s, sp_r, acc) = refs[:24]
+     sel, mt, m, pf, g,
+     ids_s, ids_r, lab, glab, cnt_s, cnt_r, sp_s, sp_r, acc) = refs[:20]
     bits = log2(n_cent)
-    rs_out = refs[24 : 24 + bits]
-    rs_in = refs[24 + bits : 24 + 2 * bits]
+    chunks = len(widths)
+    starts = [sum(widths[:c]) for c in range(chunks)]
+    lists = [refs[20 + k * chunks : 20 + (k + 1) * chunks] for k in range(4 + 2 * bits)]
+    send, recv, cz, gr = lists[:4]
+    rs_out, rs_in = lists[4 : 4 + bits], lists[4 + bits :]
     (a_ss, a_rs, rs_ss, rs_rs, ag_ss, ag_rs, g_ss, g_rs,
-     id_ss, id_rs, lab_ss, lab_rs, cnt_ss, cnt_rs, gl_ss, gl_rs, sp_ss, sp_rs) = refs[24 + 2 * bits :]
-    chunks = width // w
+     id_ss, id_rs, lab_ss, lab_rs, cnt_ss, cnt_rs, gl_ss, gl_rs, sp_ss, sp_rs) = refs[20 + (4 + 2 * bits) * chunks :]
     group = n_cent * fine
     live = bits + 1
     rows2 = n_cent * cap2
@@ -116,13 +117,13 @@
         mine = lab.at[at8(place)]
         go(mine, mine, lab_ss.at[j], lab_rs.at[j], z=cent_peer(j))
     def prepare(c):
-        moved = jnp.dot(sel[...], points[:, pl.ds(c * w, w)], preferred_element_type=F32)
-        send[c] = moved.astype(BF16)
-        recv[c, span(me, cap), :] = send[c, span(me, cap), :]
+        moved = jnp.dot(sel[...], points[:, pl.ds(starts[c], widths[c])], preferred_element_type=F32)
+        send[c][...] = moved.astype(BF16)
+        recv[c][span(me, cap), :] = send[c][span(me, cap), :]
 
     def dispatch(c):
         for j in range(1, n_dp):
-            go(send.at[c, span(dp_peer(j), cap)], recv.at[c, span(me, cap)],
+            go(send[c].at[span(dp_peer(j), cap)], recv[c].at[span(me, cap)],
                a_ss.at[c, j], a_rs.at[c, j], d=dp_peer(j))
 
     prepare(0)
@@ -136,10 +137,9 @@
     for j in range(1, n_dp):
         go(ids_s.at[at8(dp_peer(j))], ids_r.at[at8(me)], id_ss.at[j], id_rs.at[j], d=dp_peer(j))
     ids_r[at8(me), :] = ids_s[at8(me), :]
-    for c in range(1, chunks):
+    for c in range(1, min(AHEAD, chunks)):
         prepare(c)
-        if c < AHEAD:
-            dispatch(c)
+        dispatch(c)
 
     for j in range(1, n_cent):
         copy(lab.at[at8(place)], lab.at[at8(reverse(cent_peer(n_cent - j)))],
@@ -216,43 +216,45 @@
         return (place // size) * size
 
     def rs_parts(c, b):
-        return (rs_out[b].at[c], rs_in[b].at[c], rs_ss.at[c, b], rs_rs.at[c, b])
+        return (rs_out[b][c], rs_in[b][c], rs_ss.at[c, b], rs_rs.at[c, b])
 
     def rs_send(c, b):
         half = n_cent >> (b + 1)
         other = 2 * keep(b) + half - keep(b + 1)
-        rs_out[b][c] = pf[c % live, pl.ds(pl.multiple_of(other * fine, fine), half * fine), :].astype(BF16)
+        theirs = pl.ds(pl.multiple_of(other * fine, fine), half * fine)
+        rs_out[b][c][...] = pf[c % live, theirs, : widths[c]].astype(BF16)
         go(*rs_parts(c, b), z=cent_partner(b))
 
     def rs_add(c, b):
         half = n_cent >> (b + 1)
         copy(*rs_parts(c, b), z=cent_partner(b)).wait_recv()
         mine = pl.ds(pl.multiple_of(keep(b + 1) * fine, fine), half * fine)
-        pf[c % live, mine, :] += rs_in[b][c].astype(F32)
+        pf[c % live, mine, : widths[c]] += rs_in[b][c][...].astype(F32)
 
     def ag_send(c):
-        mine = cz.at[c, span(place, fine)]
+        mine = cz[c].at[span(place, fine)]
         for j in range(1, n_cent):
             go(mine, mine, ag_ss.at[c, j], ag_rs.at[c, j], z=cent_peer(j))
 
     def ag_wait(c):
         for j in range(1, n_cent):
             source = cent_peer(n_cent - j)
-            theirs = cz.at[c, span(reverse(source), fine)]
+            theirs = cz[c].at[span(reverse(source), fine)]
             copy(theirs, theirs, ag_ss.at[c, j], ag_rs.at[c, j], z=source).wait_recv()
 
     def sums(c):
         for j in range(1, n_dp):
             source = dp_peer(n_dp - j)
-            copy(send.at[c, span(me, cap)], recv.at[c, span(source, cap)],
+            copy(send[c].at[span(me, cap)], recv[c].at[span(source, cap)],
                  a_ss.at[c, j], a_rs.at[c, j], d=source).wait_recv()
         if c + AHEAD < chunks:
+            prepare(c + AHEAD)
             dispatch(c + AHEAD)
         if cap % 128 == 0:
-            pf[c % live] = jnp.dot(m[...], recv[c], preferred_element_type=F32)
+            pf[c % live, :, : widths[c]] = jnp.dot(m[...], recv[c][...], preferred_element_type=F32)
         else:
-            pf[c % live] = lax.dot_general(mt[...], recv[c], (((0,), (0,)), ((), ())),
-                                    preferred_element_type=F32)
+            pf[c % live, :, : widths[c]] = lax.dot_general(
+                mt[...], recv[c][...], (((0,), (0,)), ((), ())), preferred_element_type=F32)
         rs_send(c, 0)
 
     def halve(b, c):
@@ -261,13 +263,13 @@
 
     def centroids(c):
         rs_add(c, bits - 1)
-        value = (pf[c % live, span(place, fine), :] / fine_scale).astype(BF16)
-        cz[c, span(place, fine), :] = value
-        fine_out[:, pl.ds(c * w, w)] = value
+        value = (pf[c % live, span(place, fine), : widths[c]] / fine_scale).astype(BF16)
+        cz[c][span(place, fine), :] = value
+        fine_out[:, pl.ds(starts[c], widths[c])] = value
         ag_send(c)
 
     def g_rows(c, d):
-        return gr.at[c, span(d, rows2)]
+        return gr[c].at[span(d, rows2)]
 
     def g_args(c, k, d):
         return (g_rows(c, d), g_rows(c, d), g_ss.at[c, k], g_rs.at[c, k])
@@ -282,10 +284,8 @@
 
     def pick_rows(c):
         ag_wait(c)
-        mine = jnp.zeros((rows2, w), F32)
-        for k in range(n_cent):
-            mine = mine + jnp.dot(pick[k], cz[c, pl.ds(k * fine, fine), :], preferred_element_type=F32)
-        gr[c, span(me, rows2), :] = mine.astype(BF16)
+        mine = jnp.dot(jnp.concatenate(pick, axis=1), cz[c][...], preferred_element_type=F32)
+        gr[c][span(me, rows2), :] = mine.astype(BF16)
         if n_dp == 8:
             go(*g_args(c, 0, me), d=me + d1)
             go(*g_args(c, 1, me), d=me + d2)
@@ -293,9 +293,11 @@
         else:
             for j in range(1, n_dp):
                 go(*g_args(c, j, me), d=dp_peer(j))
-        near = jnp.dot(mt[...], cz[c], preferred_element_type=F32)
-        gap = jnp.square(recv[c].astype(F32) - near)
-        acc[...] += sum(gap[:, i : i + 128] for i in range(0, w, 128))
+
+    def spreads(c):
+        near = jnp.dot(mt[...], cz[c][...], preferred_element_type=F32)
+        gap = jnp.square(recv[c][...].astype(F32) - near)
+        acc[...] += sum(gap[:, i : i + 128] for i in range(0, widths[c], 128))
         if c == chunks - 1:
             for k in range(n_dp):
                 col = jnp.sum(acc[pl.ds(k * cap, cap), :], axis=1, keepdims=True) / width
@@ -327,14 +329,15 @@
             for j in range(1, n_dp):
                 source = dp_peer(n_dp - j)
                 copy(*g_args(c, j, source), d=source).wait_recv()
-        result = jnp.dot(g[...], gr[c], preferred_element_type=F32)
-        coarse_out[:, pl.ds(c * w, w)] = (result / coarse_scale).astype(BF16)
+        result = jnp.dot(g[...], gr[c][...], preferred_element_type=F32)
+        coarse_out[:, pl.ds(starts[c], widths[c])] = (result / coarse_scale).astype(BF16)
 
     stages = [sums]
     stages += [functools.partial(halve, b) for b in range(1, bits)]
     stages += [centroids]
-    stages += [pick_rows, forward_one, forward_two, finish]
-    for tick in range(chunks + len(stages) - 1):
+    stages += [pick_rows, forward_one, forward_two]
+    late = [(len(stages) - 3, spreads), (len(stages), finish)]
+    for tick in range(chunks + len(stages)):
         for s in reversed(range(len(stages))):
             if 0 <= tick - s < chunks:
                 stages[s](tick - s)
@@ -342,6 +345,9 @@
             fine_scale = fine_counts()
         if tick == 1:
             coarse_scale = coarse_members()
+        for s, stage in late:
+            if 0 <= tick - s < chunks:
+                stage(tick - s)
 
     for j in range(1, n_dp):
         source = dp_peer(n_dp - j)
@@ -390,21 +396,20 @@
     cap = max(2, 2 * p_rows // sources) * n_cent
     cap2 = max(2, 2 * fine // n_cent)
     block = COARSE // n_cent
-    w = width // CHUNKS
+    parts = (1, 2, 2, 2, 1) if n_cent == 4 else (1,) * 8
+    widths = tuple(width // 8 * part for part in parts)
+    chunks = len(widths)
     bits = log2(n_cent)
     group, slots, rows2, lanes = n_cent * fine, n_dp * cap, n_cent * cap2, max(cap, 128)
-    cfg = (n_dp, n_cent, p_rows, fine, width, w, cap, cap2, block)
-    halves = [pltpu.VMEM((CHUNKS, (n_cent >> (b + 1)) * fine, w), BF16) for b in range(bits)]
+    cfg = (n_dp, n_cent, p_rows, fine, width, widths, cap, cap2, block)
+    half_rows = [(n_cent >> (b + 1)) * fine for b in range(bits)]
+    heights = [slots, slots, group, n_dp * rows2, *half_rows, *half_rows]
     dma = pltpu.SemaphoreType.DMA
     scratch = [
         pltpu.VMEM((slots, p_rows), BF16),
-        pltpu.VMEM((CHUNKS, slots, w), BF16),
-        pltpu.VMEM((CHUNKS, slots, w), BF16),
         pltpu.VMEM((slots, group), BF16),
         pltpu.VMEM((group, slots) if cap % 128 == 0 else (16, 128), BF16),
-        pltpu.VMEM((bits + 1, group, w), F32),
-        pltpu.VMEM((CHUNKS, group, w), BF16),
-        pltpu.VMEM((CHUNKS, n_dp * rows2, w), BF16),
+        pltpu.VMEM((bits + 1, group, max(widths)), F32),
         pltpu.VMEM((block, n_dp * rows2), BF16),
         pltpu.VMEM((n_dp * 8, lanes), F32),
         pltpu.VMEM((n_dp * 8, lanes), F32),
@@ -415,12 +420,11 @@
         pltpu.VMEM((n_dp * 8, lanes), F32),
         pltpu.VMEM((n_dp * 8, lanes), F32),
         pltpu.VMEM((slots, 128), F32),
-        *halves,
-        *halves,
-        dma((CHUNKS, n_dp)), dma((CHUNKS, n_dp)),
-        dma((CHUNKS, bits)), dma((CHUNKS, bits)),
-        dma((CHUNKS, n_cent)), dma((CHUNKS, n_cent)),
-        dma((CHUNKS, n_dp)), dma((CHUNKS, n_dp)),
+        *(pltpu.VMEM((height, w), BF16) for height in heights for w in widths),
+        dma((chunks, n_dp)), dma((chunks, n_dp)),
+        dma((chunks, bits)), dma((chunks, bits)),
+        dma((chunks, n_cent)), dma((chunks, n_cent)),
+        dma((chunks, n_dp)), dma((chunks, n_dp)),
         dma((n_dp,)), dma((n_dp,)),
         dma((n_cent,)), dma((n_cent,)),
         dma((n_cent,)), dma((n_cent,)),

time: 84 us -> 90.8 us (1.081); the launches traced: 83.8 us -> 89.1 us
  Pallas kernels: 83 us -> 88.3 us
    pallas_call x1, Pallas kernels: 80.5 us -> 85.8 us  [body(): pl.pallas_call(functools.partial(kernel, cfg), out_shape=(jax.ShapeDtypeS...]
where the time goes in v4:
time: 90.8 us; the launch traced here: 89.1 us
  Pallas kernels  88.3 us (97%)
    pallas_call x1, Pallas kernels, body(): pl.pallas_call(functools.partial(kernel, cfg), out_shape=(jax.ShapeDtypeS...  85.8 us
    pallas_call x1, Pallas kernels, body(): pl.pallas_call(place_results, out_shape=tuple((jax.ShapeDtypeStruct(r.sha...  2.54 us

profile of v4, /device:TPU:1, one launch (start us, length us, event | category | flops | bytes accessed | tf_op | source)
XLA Modules:
  0.0 89.1 jit_solution(12736608247077762214)
XLA Ops:
  0.6 85.8 %shard_map.58 = (f32[1,512]{1,0:T(1,128)}, bf16[128,1024]{1,0:T(8,128)(2,1)}, bf16[1024,1024]{1,0:T(8,128)(2,1)}) custom-call(bf16[512,1024]{1,0:T(8,128)(2,1)} %refs_0_.1, s32[1,512]{1,0:T(1,128)} %bitcast.3, s32[1,128]{1,0:T(1,128)} %bitcast.5), custom_call_target="tpu_custom_call" | custom-call | flops 7516192768 | bytes 3407872 | tf_op jit(solution)/shard_map/pallas_call | solution.py:435
  86.4 2.5 %shard_map.59 = (f32[1,512]{1,0:T(1,128)}, bf16[128,1024]{1,0:T(8,128)(2,1)}, bf16[1024,1024]{1,0:T(8,128)(2,1)}) custom-call(f32[1,512]{1,0:T(1,128)} %get-tuple-element.9.refs_0_, bf16[128,1024]{1,0:T(8,128)(2,1)} %get-tuple-element.10.refs_1_, bf16[1024,1024]{1,0:T(8,128)(2,1)} %get-tuple-element.11.refs_2_), custom_call_target="tpu_custom_call" | custom-call | tf_op jit(solution)/shard_map/pallas_call | solution.py:455

commit v5 on v4

--- a/solution.py
+++ b/solution.py
@@ -8,7 +8,7 @@
 from jax.sharding import PartitionSpec as P
 
 COARSE = 4096
-AHEAD = 4
+AHEAD = 3
 PARTS = 4
 MESH = pl.DeviceIdType.MESH
 F32 = jnp.float32
@@ -396,7 +396,7 @@
     cap = max(2, 2 * p_rows // sources) * n_cent
     cap2 = max(2, 2 * fine // n_cent)
     block = COARSE // n_cent
-    parts = (1, 2, 2, 2, 1) if n_cent == 4 else (1,) * 8
+    parts = (1,) * 8
     widths = tuple(width // 8 * part for part in parts)
     chunks = len(widths)
     bits = log2(n_cent)

time: 90.8 us -> 87.5 us (0.964)
  Pallas kernels: 88.3 us -> 85 us
    pallas_call x1, Pallas kernels: 85.8 us -> 82.4 us  [body(): pl.pallas_call(functools.partial(kernel, cfg), out_shape=(jax.ShapeDtypeS...]
where the time goes in v5:
time: 87.5 us; the launch traced here: 85.8 us
  Pallas kernels  85 us (97%)
    pallas_call x1, Pallas kernels, body(): pl.pallas_call(functools.partial(kernel, cfg), out_shape=(jax.ShapeDtypeS...  82.4 us
    pallas_call x1, Pallas kernels, body(): pl.pallas_call(place_results, out_shape=tuple((jax.ShapeDtypeStruct(r.sha...  2.54 us

profile of v5, /device:TPU:1, one launch (start us, length us, event | category | flops | bytes accessed | tf_op | source)
XLA Modules:
  0.0 85.8 jit_solution(1418235287110901515)
XLA Ops:
  0.6 82.4 %shard_map.58 = (f32[1,512]{1,0:T(1,128)}, bf16[128,1024]{1,0:T(8,128)(2,1)}, bf16[1024,1024]{1,0:T(8,128)(2,1)}) custom-call(bf16[512,1024]{1,0:T(8,128)(2,1)} %refs_0_.1, s32[1,512]{1,0:T(1,128)} %bitcast.3, s32[1,128]{1,0:T(1,128)} %bitcast.5), custom_call_target="tpu_custom_call" | custom-call | flops 7516192768 | bytes 3407872 | tf_op jit(solution)/shard_map/pallas_call | solution.py:435
  83.1 2.5 %shard_map.59 = (f32[1,512]{1,0:T(1,128)}, bf16[128,1024]{1,0:T(8,128)(2,1)}, bf16[1024,1024]{1,0:T(8,128)(2,1)}) custom-call(f32[1,512]{1,0:T(1,128)} %get-tuple-element.9.refs_0_, bf16[128,1024]{1,0:T(8,128)(2,1)} %get-tuple-element.10.refs_1_, bf16[1024,1024]{1,0:T(8,128)(2,1)} %get-tuple-element.11.refs_2_), custom_call_target="tpu_custom_call" | custom-call | tf_op jit(solution)/shard_map/pallas_call | solution.py:455

commit v6 on v3

--- a/solution.py
+++ b/solution.py
@@ -9,7 +9,7 @@
 
 COARSE = 4096
 CHUNKS = 8
-AHEAD = 3
+AHEAD = 2
 PARTS = 4
 MESH = pl.DeviceIdType.MESH
 F32 = jnp.float32

time: 84 us -> 84 us (level)
  no operation moved by 1% of the time
where the time goes in v6:
time: 84 us; the launch traced here: 83.8 us
  Pallas kernels  83 us (99%)
    pallas_call x1, Pallas kernels, body(): pl.pallas_call(functools.partial(kernel, cfg), out_shape=(jax.ShapeDtypeS...  80.5 us
    pallas_call x1, Pallas kernels, body(): pl.pallas_call(place_results, out_shape=tuple((jax.ShapeDtypeStruct(r.sha...  2.54 us

profile of v6, /device:TPU:1, one launch (start us, length us, event | category | flops | bytes accessed | tf_op | source)
XLA Modules:
  0.0 83.8 jit_solution(7535647830381083679)
XLA Ops:
  0.6 80.5 %shard_map.58 = (f32[1,512]{1,0:T(1,128)}, bf16[128,1024]{1,0:T(8,128)(2,1)}, bf16[1024,1024]{1,0:T(8,128)(2,1)}) custom-call(bf16[512,1024]{1,0:T(8,128)(2,1)} %refs_0_.1, s32[1,512]{1,0:T(1,128)} %bitcast.3, s32[1,128]{1,0:T(1,128)} %bitcast.5), custom_call_target="tpu_custom_call" | custom-call | flops 7516192768 | bytes 3407872 | tf_op jit(solution)/shard_map/pallas_call | solution.py:431
  81.1 2.5 %shard_map.59 = (f32[1,512]{1,0:T(1,128)}, bf16[128,1024]{1,0:T(8,128)(2,1)}, bf16[1024,1024]{1,0:T(8,128)(2,1)}) custom-call(f32[1,512]{1,0:T(1,128)} %get-tuple-element.9.refs_0_, bf16[128,1024]{1,0:T(8,128)(2,1)} %get-tuple-element.10.refs_1_, bf16[1024,1024]{1,0:T(8,128)(2,1)} %get-tuple-element.11.refs_2_), custom_call_target="tpu_custom_call" | custom-call | tf_op jit(solution)/shard_map/pallas_call | solution.py:451
